TPU v7x, 32 devices: a whole 2x2x4 slice. The times are simulated.
32 devices in a mesh: ctx: 16 (over z, x, core), chan: 2 (over y).
Axes of the slice: x: 2, y: 2, z: 4, core: 2. Of those that a mesh axis runs over, the one named last changes fastest.
Arguments:
- raw_query: bfloat16 [4096, 4096], P('ctx', 'chan'), may hold values from -6 to 6
- raw_key: bfloat16 [4096, 4096], P('ctx', 'chan'), may hold values from -6 to 6
- raw_value: bfloat16 [4096, 4096], P('ctx', 'chan'), may hold values from -6 to 6
- short_filter: float32 [3, 3, 4096], P(None, None, 'chan'), may hold values from -3 to 3
- long_filter: float32 [4096, 4096], P('ctx', 'chan'), may hold values from -6 to 6
- skip: float32 [4096], P('chan'), may hold values from -1 to 1
- w_out: bfloat16 [4096, 8192], P('chan'), may hold values from -0.125 to 0.125
Outputs:
- output: bfloat16 [4096, 8192], P('ctx', 'chan')
All inputs are finite; a program needn't handle non-finite values.
Results may differ from a plain program's by a relative error of at most 0.005.
Values may be sent and summed in bfloat16 or wider, within the bound.
A program may use at most 256 MiB of HBM per device.

v0:
```python
import math

import jax
import jax.numpy as jnp
import numpy as np
from jax import lax
from jax.sharding import PartitionSpec as P

three_pass = lax.Precision.HIGH


def passed_along(value, axis, steps):
    count = lax.axis_size(axis)
    first, last = (max(0, -steps), min(count, count - steps))
    return lax.ppermute(value, axis, [(source, source + steps) for source in range(first, last)])


def outer_table(outer):
    half = outer // 2
    angle = 2.0 * np.pi / outer * (np.outer(np.arange(half + 1), np.arange(half)) % outer)
    return np.concatenate([np.cos(angle), -np.sin(angle)], axis=0).astype(np.float32)


def inner_tables(outer, inner):
    total = outer * inner
    k1 = np.arange(outer // 2 + 1)[:, None, None]
    k2 = np.arange(inner)[None, :, None]
    n2 = np.arange(inner)[None, None, :]
    angle = 2.0 * np.pi / total * (n2 * (k1 + outer * k2) % total)
    c, s = np.cos(angle), np.sin(angle)
    top = np.concatenate([c, s], axis=2)
    low = np.concatenate([-s, c], axis=2)
    return np.concatenate([top, low], axis=1).astype(np.float32)


def local_convolution(signal, kernel):
    length, width = signal.shape
    inner = 128
    outer = 2 * length // inner
    half = outer // 2
    first = jnp.asarray(outer_table(outer))
    second = jnp.asarray(inner_tables(outer, inner))
    both = jnp.concatenate([signal, kernel], axis=1).astype(jnp.float32)
    both = both.reshape(half, inner, 2 * width)
    spread = jnp.einsum("kn,nmc->kmc", first, both, precision=three_pass)
    spread = jnp.concatenate([spread[: half + 1], spread[half + 1 :]], axis=1)
    spectrum = jnp.einsum("kpq,kqc->kpc", second, spread, precision=three_pass)
    real, imag = spectrum[:, :inner], spectrum[:, inner:]
    xr, hr = real[..., :width], real[..., width:]
    xi, hi = imag[..., :width], imag[..., width:]
    product = jnp.concatenate([xr * hr - xi * hi, xr * hi + xi * hr], axis=1)
    back = jnp.einsum("kpq,kpc->kqc", second, product, precision=three_pass)
    stacked = jnp.concatenate([back[:, :inner], back[:, inner:]], axis=0)
    weight = np.full((half + 1,), 2.0)
    weight[0] = weight[-1] = 1.0
    scale = np.concatenate([weight, weight])[:, None] / (2 * length)
    last = jnp.asarray((outer_table(outer) * scale).astype(np.float32))
    rows = jnp.einsum("kn,kmc->nmc", last, stacked, precision=three_pass)
    return rows.reshape(length, width)


def local(raw_query, raw_key, raw_value, short_filter, long_filter, skip, w_out):
    raw_list = [raw.astype(jnp.float32) for raw in (raw_query, raw_key, raw_value)]
    width = raw_list[0].shape[1]
    tail_rows = jnp.concatenate([raw_list[0][-2:], raw_list[1][-2:], raw_list[2][-2:]], axis=1)
    before = passed_along(tail_rows, "ctx", 1)
    filtered = []
    for branch in range(3):
        padded = jnp.concatenate(
            [before[:, branch * width : (branch + 1) * width], raw_list[branch]], axis=0
        )
        filtered.append(
            short_filter[branch, 0] * padded[2:]
            + short_filter[branch, 1] * padded[1:-1]
            + short_filter[branch, 2] * padded[:-2]
        )
    queries, key_rows, value_rows = filtered
    mixed = key_rows * value_rows
    kernel = lax.all_to_all(
        long_filter.astype(jnp.bfloat16), "ctx", split_axis=1, concat_axis=0, tiled=True
    )
    signal = lax.all_to_all(
        mixed.astype(jnp.bfloat16), "ctx", split_axis=1, concat_axis=0, tiled=True
    )
    convolved = local_convolution(signal, kernel).astype(jnp.bfloat16)
    convolved = lax.all_to_all(convolved, "ctx", split_axis=0, concat_axis=1, tiled=True)
    gated = (queries * (convolved.astype(jnp.float32) + skip * mixed)).astype(jnp.bfloat16)
    count = lax.axis_size("chan")
    me = lax.axis_index("chan")
    features = w_out.shape[1] // count

    def share(owner):
        columns = lax.dynamic_slice_in_dim(w_out, owner * features, features, axis=1)
        return jnp.dot(gated, columns, preferred_element_type=jnp.float32)

    arrived = []
    for step in range(1, count):
        pairs = [(source, (source + step) % count) for source in range(count)]
        arrived.append(lax.ppermute(share((me + step) % count).astype(jnp.bfloat16), "chan", pairs))
    summed = share(me)
    for part in arrived:
        summed = summed + part.astype(jnp.float32)
    return summed.astype(jnp.bfloat16)


def solution(mesh):
    in_specs = (
        P("ctx", "chan"),
        P("ctx", "chan"),
        P("ctx", "chan"),
        P(None, None, "chan"),
        P("ctx", "chan"),
        P("chan"),
        P("chan", None),
    )
    out_specs = P("ctx", "chan")
    return jax.shard_map(local, mesh=mesh, in_specs=in_specs, out_specs=out_specs, check_vma=False)
```

profile of v0, /device:TPU:0, one launch (start us, length us, event | category | flops | bytes accessed | tf_op | source)
XLA Modules:
  0.0 240.5 jit_solution(12002841913401468341)
XLA Ops:
  0.0 2.6 %copy.43 = bf16[256,2048]{0,1:T(8,128)(2,1)} copy(f32[256,2048]{1,0:T(8,128)} %param.14) | data formatting | bytes 3145728 | tf_op args[4]
  2.6 7.4 %all-to-all-start.1 = ((bf16[256,16,128]{0,2,1:T(8,128)(2,1)}), bf16[256,16,128]{0,2,1:T(8,128)(2,1)}, u32[]{:S(2)}, u32[]{:S(2)}) async-start(bf16[256,16,128]{0,2,1:T(8,128)(2,1)} %bitcast.13), calls=%async_computation.1 | async-start | bytes 2097152 | tf_op jit(solution)/shard_map/all_to_all | solution.py:79
  10.1 0.5 copy.33
  10.6 0.2 slice.122
  10.8 0.3 copy.36
  11.1 0.1 copy-done.4
  11.3 0.5 copy.34
  11.8 0.2 slice.123
  12.0 0.3 copy.37
  12.4 1.5 copy.35
  13.9 1.2 slice.124
  15.1 1.6 copy.38
  16.7 2.3 collective-permute-start
  18.9 0.1 fusion.53
  19.0 1.5 convert_element_type.48
  20.5 1.5 convert_element_type.49
  22.0 1.4 copy.40
  23.3 1.4 copy.41
  24.7 9.5 %fusion.49 = (bf16[256,2048]{0,1:T(8,128)(2,1)}, f32[256,2048]{0,1:T(8,128)}) fusion(f32[256,2048]{0,1:T(8,128)} %convert_element_type.49, f32[2,2048]{0,1:T(8,128)} %copy.41, f32[2048]{0:T(1024)S(1)} %bitcast.40, f32[2048]{0:T(1024)S(1)} %bitcast.41, f32[2048]{0:T(1024)S(1)} %bitcast.36, f32[256,2048]{0,1:T(8,128)S(1)} %copy-done, f32[2,2048]{0,1:T(8,128)} %copy.40, ...), kind=kLoop, calls=%fused_computation.58 | loop fusion | flops 8388608 | bytes 7421952 | tf_op jit(solution)/shard_map/convert_element_type | solution.py:83
  34.2 18.0 %all-to-all-start = ((bf16[256,16,128]{0,2,1:T(8,128)(2,1)}), bf16[256,16,128]{0,2,1:T(8,128)(2,1)S(1)}, u32[]{:S(2)}, u32[]{:S(2)}) async-start(bf16[256,16,128]{0,2,1:T(8,128)(2,1)} %bitcast.32), calls=%async_computation | async-start | bytes 2097152 | tf_op jit(solution)/shard_map/all_to_all | solution.py:82
  52.2 1.6 copy.44
  53.8 1.6 copy.46
  55.5 19.7 %all-to-all-done = bf16[256,16,128]{0,2,1:T(8,128)(2,1)S(1)} async-done(((bf16[256,16,128]{0,2,1:T(8,128)(2,1)}), bf16[256,16,128]{0,2,1:T(8,128)(2,1)S(1)}, u32[]{:S(2)}, u32[]{:S(2)}) %all-to-all-start) | async-done | bytes 1048608 | tf_op jit(solution)/shard_map/all_to_all | solution.py:82
  75.1 0.8 copy.42
  76.0 0.7 copy.45
  76.7 0.5 copy-done.2
  77.2 2.6 %fusion.33 = f32[66,128,256]{2,0,1:T(8,128)S(1)} fusion(f32[66,32,1]{0,1,2:T(8,128)S(1)} %copy-done.7, bf16[32,128,128]{2,0,1:T(8,128)(2,1)S(1)} %copy-done.2, bf16[32,128,128]{2,0,1:T(8,128)(2,1)S(1)} %copy.45), kind=kOutput, calls=%fused_computation.45 | convolution fusion | flops 419430400 | bytes 10756352 | tf_op jit(solution)/shard_map/kn,nmc->kmc/dot_general | solution.py:45
  79.9 4.9 %fusion.51 = (f32[33,128,256]{2,0,1:T(8,128)}, f32[33,128,256]{2,0,1:T(8,128)}) fusion(f32[66,128,256]{2,0,1:T(8,128)S(1)} %fusion.33), kind=kLoop, calls=%fused_computation.59 | loop fusion | bytes 17301504 | tf_op jit(solution)/shard_map/slice | solution.py:46
  84.8 8.7 %pad_maximum_fusion = f32[33,256,256]{2,0,1:T(8,128)} fusion(f32[33,128,256]{2,0,1:T(8,128)} %get-tuple-element.8, f32[33,128,256]{2,0,1:T(8,128)} %get-tuple-element.7), kind=kLoop, calls=%fused_computation.4 | loop fusion | flops 2162688 | bytes 17301504 | tf_op jit(solution)/shard_map/concatenate | solution.py:46
  93.5 16.3 %fusion.4 = f32[33,256,256]{2,1,0:T(8,128)} fusion(f32[33,256,256]{2,1,0:T(8,128)} %constant.30.clone, f32[33,256,256]{2,0,1:T(8,128)} %pad_maximum_fusion), kind=kOutput, calls=%fused_computation.5 | convolution fusion | flops 3321888768 | bytes 25952256 | tf_op jit(solution)/shard_map/kpq,kqc->kpc/dot_general | solution.py:47
  109.8 4.8 %multiply_subtract_fusion = (f32[33,128,128]{2,1,0:T(8,128)S(1)}, f32[33,128,128]{2,1,0:T(8,128)S(1)}) fusion(f32[33,256,256]{2,1,0:T(8,128)} %fusion.4), kind=kLoop, calls=%fused_computation.23 | loop fusion | flops 3244032 | bytes 12976128 | tf_op jit(solution)/shard_map/sub | solution.py:51
  114.6 10.0 %fusion.11 = f32[33,256,128]{2,1,0:T(8,128)S(1)} fusion(f32[33,256,256]{2,1,0:T(8,128)} %constant.30.clone, f32[33,128,128]{2,1,0:T(8,128)S(1)} %get-tuple-element.10, f32[33,128,128]{2,1,0:T(8,128)S(1)} %get-tuple-element.9), kind=kOutput, calls=%fused_computation.10 | convolution fusion | flops 1662025728 | bytes 17301504 | tf_op jit(solution)/shard_map/kpq,kpc->kqc/dot_general | solution.py:52
  124.7 0.5 fusion.52
  125.2 0.3 pad_maximum_fusion.1
  125.5 0.4 copy-done.6
  125.9 3.9 %fusion.40 = bf16[32,128,128]{2,0,1:T(8,128)(2,1)S(1)} fusion(f32[66,32,1]{0,1,2:T(8,128)S(1)} %copy-done.6, f32[66,128,128]{2,1,0:T(8,128)S(1)} %pad_maximum_fusion.1), kind=kOutput, calls=%fused_computation.52 | convolution fusion | flops 208142336 | bytes 5382400 | tf_op jit(solution)/shard_map/kn,kmc->nmc/dot_general | solution.py:58
  129.8 1.4 copy.50
  131.2 6.9 %all-to-all-start.2 = ((bf16[16,256,128]{2,1,0:T(8,128)(2,1)}), bf16[16,256,128]{2,1,0:T(8,128)(2,1)S(1)}, u32[]{:S(2)}, u32[]{:S(2)}) async-start(bf16[16,256,128]{2,1,0:T(8,128)(2,1)} %bitcast.18), calls=%async_computation.2 | async-start | bytes 2097152 | tf_op jit(solution)/shard_map/all_to_all | solution.py:86
  138.1 1.5 convert_element_type.47
  139.6 1.4 copy.39
  141.0 20.1 %all-to-all-done.2 = bf16[16,256,128]{2,1,0:T(8,128)(2,1)S(1)} async-done(((bf16[16,256,128]{2,1,0:T(8,128)(2,1)}), bf16[16,256,128]{2,1,0:T(8,128)(2,1)S(1)}, u32[]{:S(2)}, u32[]{:S(2)}) %all-to-all-start.2) | async-done | bytes 1048608 | tf_op jit(solution)/shard_map/all_to_all | solution.py:86
  161.1 0.2 convert_bitcast_fusion
  161.3 1.8 copy.51
  163.1 6.0 %fusion.29 = bf16[256,2048]{0,1:T(8,128)(2,1)S(1)} fusion(f32[2,2048]{0,1:T(8,128)S(1)} %copy-done.1, f32[256,2048]{0,1:T(8,128)} %convert_element_type.47, f32[256,16,128]{0,2,1:T(8,128)} %copy.51, f32[256,2048]{0,1:T(8,128)} %get-tuple-element.6, f32[2048]{0:T(1024)S(1)} %copy-done.8, f32[2048]{0:T(1024)S(1)} %bitcast.43, f32[2048]{0:T(1024)S(1)} %bitcast.44, ...), kind=kLoop, calls=%fused_computation.38 | loop fusion | flops 5767168 | bytes 7389184 | tf_op jit(solution)/shard_map/convert_element_type | solution.py:87
  169.2 11.5 %fusion.6 = bf16[256,4096]{1,0:T(8,128)(2,1)} fusion(bf16[256,2048]{0,1:T(8,128)(2,1)S(1)} %fusion.29, bf16[2048,8192]{1,0:T(8,128)(2,1)} %param.16, s32[]{:T(128)S(6)} %select_n.15), kind=kOutput, calls=%fused_computation.7 | convolution fusion | flops 4296015872 | bytes 19922948 | tf_op jit(solution)/shard_map/dot_general | solution.py:94
  180.7 1.5 collective-permute-start.1
  182.2 46.8 %collective-permute-done.1 = bf16[256,4096]{1,0:T(8,128)(2,1)S(1)} collective-permute-done((bf16[256,4096]{1,0:T(8,128)(2,1)}, bf16[256,4096]{1,0:T(8,128)(2,1)S(1)}, u32[]{:S(2)}, u32[]{:S(2)}) %collective-permute-start.1) | collective-permute-done | bytes 2097184 | tf_op jit(solution)/shard_map/ppermute | solution.py:99
  229.0 11.5 %add_convert_fusion = bf16[256,4096]{1,0:T(8,128)(2,1)} fusion(bf16[256,4096]{1,0:T(8,128)(2,1)S(1)} %collective-permute-done.1, bf16[256,2048]{0,1:T(8,128)(2,1)S(1)} %fusion.29, bf16[2048,8192]{1,0:T(8,128)(2,1)} %param.16, s32[]{:T(128)S(6)} %select_n.13), kind=kOutput, calls=%fused_computation.15 | convolution fusion | flops 4298113024 | bytes 22020100 | tf_op jit(solution)/shard_map/dot_general | solution.py:94
  (19 shorter events, 0.1 us)
Async XLA Ops:
  0.0 10.1 %copy-start.3 = (bf16[256,2048]{1,0:T(8,128)(2,1)S(1)}, bf16[256,2048]{1,0:T(8,128)(2,1)}, u32[]{:S(2)}) copy-start(bf16[256,2048]{1,0:T(8,128)(2,1)} %param.10) | copy-start | bytes 3145732
  2.6 31.6 %all-to-all-start.1 = ((bf16[256,16,128]{0,2,1:T(8,128)(2,1)}), bf16[256,16,128]{0,2,1:T(8,128)(2,1)}, u32[]{:S(2)}, u32[]{:S(2)}) async-start(bf16[256,16,128]{0,2,1:T(8,128)(2,1)} %bitcast.13), calls=%async_computation.1 | async-start | bytes 2097152 | tf_op jit(solution)/shard_map/all_to_all | solution.py:79
  10.1 1.2 copy-start.4
  12.4 6.6 %copy-start.5 = (f32[3,3,2048]{2,1,0:T(4,128)S(1)}, f32[3,3,2048]{2,1,0:T(4,128)}, u32[]{:S(2)}) copy-start(f32[3,3,2048]{2,1,0:T(4,128)} %param.13) | copy-start | bytes 221188
  16.7 5.3 %collective-permute-start = (f32[2,6144]{1,0:T(2,128)S(1)}, f32[2,6144]{1,0:T(2,128)S(1)}, u32[]{:S(2)}, u32[]{:S(2)}) collective-permute-start(f32[2,6144]{1,0:T(2,128)S(1)} %pad_maximum_fusion.5), channel_id=1, source_target_pairs={{0,2},{2,4},{4,6},{6,8},{8,10},{10,12},{12,14},{14,16},{16,18},{18... | collective-permute-start | bytes 147464 | tf_op jit(solution)/shard_map/ppermute | solution.py:15
  22.0 2.8 %copy-start = (f32[256,2048]{0,1:T(8,128)S(1)}, f32[256,2048]{0,1:T(8,128)}, u32[]{:S(2)}) copy-start(f32[256,2048]{0,1:T(8,128)} %convert_element_type.48) | copy-start | bytes 6291460
  34.2 40.9 %all-to-all-start = ((bf16[256,16,128]{0,2,1:T(8,128)(2,1)}), bf16[256,16,128]{0,2,1:T(8,128)(2,1)S(1)}, u32[]{:S(2)}, u32[]{:S(2)}) async-start(bf16[256,16,128]{0,2,1:T(8,128)(2,1)} %bitcast.32), calls=%async_computation | async-start | bytes 2097152 | tf_op jit(solution)/shard_map/all_to_all | solution.py:82
  55.5 21.2 %copy-start.7 = (f32[66,32,1]{0,1,2:T(8,128)S(1)}, f32[66,32,1]{0,1,2:T(8,128)}, u32[]{:S(2)}) copy-start(f32[66,32,1]{0,1,2:T(8,128)} %constant.32) | copy-start | bytes 25348
  76.0 1.2 copy-start.2
  125.2 0.7 copy-start.6
  131.2 29.8 %all-to-all-start.2 = ((bf16[16,256,128]{2,1,0:T(8,128)(2,1)}), bf16[16,256,128]{2,1,0:T(8,128)(2,1)S(1)}, u32[]{:S(2)}, u32[]{:S(2)}) async-start(bf16[16,256,128]{2,1,0:T(8,128)(2,1)} %bitcast.18), calls=%async_computation.2 | async-start | bytes 2097152 | tf_op jit(solution)/shard_map/all_to_all | solution.py:86
  161.3 1.9 copy-start.1
  161.3 1.8 copy-start.8
  180.7 48.4 %collective-permute-start.1 = (bf16[256,4096]{1,0:T(8,128)(2,1)}, bf16[256,4096]{1,0:T(8,128)(2,1)S(1)}, u32[]{:S(2)}, u32[]{:S(2)}) collective-permute-start(bf16[256,4096]{1,0:T(8,128)(2,1)} %fusion.6), channel_id=1, source_target_pairs={{0,1},{1,0},{2,3},{3,2},{4,5},{5,4},{6,7},{7,6},{8,9},{9,8},{10,11... | collective-permute-start | bytes 6291464 | tf_op jit(solution)/shard_map/ppermute | solution.py:99
where the time goes:
time: 242 us; the launch traced here: 241 us
  waiting for transfers between devices  86.6 us (36%)
  matrix products  55.9 us (23%)
  starting transfers between devices  36 us (15%)
  other arithmetic  34.1 us (14%)
  local copies, waits for them, and re-layouts  27.7 us (11%)
    ppermute x1, waiting for transfers between devices, local(): lax.ppermute(share((me + step) % count).astype(jnp.bfloat16), 'chan', pairs)  46.8 us
    dot_general x2, matrix products, share(): return jnp.dot(gated, columns, preferred_element_type=jnp.float32)  23 us
    all_to_all x1, waiting for transfers between devices, local(): lax.all_to_all(convolved, 'ctx', split_axis=0, concat_axis=1, tiled=True)  20.1 us
    all_to_all x1, waiting for transfers between devices, local(): lax.all_to_all(mixed.astype(jnp.bfloat16), 'ctx', split_axis=1, concat_ax...  19.7 us
    all_to_all x1, starting transfers between devices, local(): lax.all_to_all(mixed.astype(jnp.bfloat16), 'ctx', split_axis=1, concat_ax...  18 us
    dot_general x1, matrix products, local_convolution(): spectrum = jnp.einsum('kpq,kqc->kpc', second, spread, precision=three_pass)  16.3 us
    dot_general x1, matrix products, local_convolution(): back = jnp.einsum('kpq,kpc->kqc', second, product, precision=three_pass)  10 us
    convert_element_type x1, other arithmetic, local(): mixed.astype(jnp.bfloat16)  9.51 us
  transfers between devices with their start and end apart: 5, of which 3 were waited for; matrix products, arithmetic and copies ran while one was open for 12% of the time, Pallas kernels for 0%

commit v1 on v0

--- a/solution.py
+++ b/solution.py
@@ -1,9 +1,12 @@
+import functools
 import math
 
 import jax
 import jax.numpy as jnp
 import numpy as np
 from jax import lax
+from jax.experimental import pallas as pl
+from jax.experimental.pallas import tpu as pltpu
 from jax.sharding import PartitionSpec as P
 
 three_pass = lax.Precision.HIGH
@@ -59,7 +62,7 @@
     return rows.reshape(length, width)
 
 
-def local(raw_query, raw_key, raw_value, short_filter, long_filter, skip, w_out):
+def plain_local(raw_query, raw_key, raw_value, short_filter, long_filter, skip, w_out):
     raw_list = [raw.astype(jnp.float32) for raw in (raw_query, raw_key, raw_value)]
     width = raw_list[0].shape[1]
     tail_rows = jnp.concatenate([raw_list[0][-2:], raw_list[1][-2:], raw_list[2][-2:]], axis=1)
@@ -103,6 +106,383 @@
     return summed.astype(jnp.bfloat16)
 
 
+MESH = pl.DeviceIdType.MESH
+LANES = 128
+INNER = 128
+TILE = 512
+
+
+def added(a, b):
+    if a is None:
+        return b
+    return a if b is None else a + b
+
+
+def taken(a, b):
+    if b is None:
+        return a
+    return -b if a is None else a - b
+
+
+def times(a, c):
+    if a is None or abs(c) < 1e-12:
+        return None
+    if abs(c - 1.0) < 1e-12:
+        return a
+    return -a if abs(c + 1.0) < 1e-12 else a * np.float32(c)
+
+
+def turned(pair, angle):
+    c, s = math.cos(angle), math.sin(angle)
+    re, im = pair
+    if re is not None and im is not None and abs(abs(c) - abs(s)) < 1e-12:
+        c0 = abs(c)
+        sc, ss = (1 if c > 0 else -1), (1 if s > 0 else -1)
+        plus, minus = (re + im) * np.float32(c0), (re - im) * np.float32(c0)
+        real = minus if sc == ss else plus
+        imag = plus if sc == ss else minus
+        return (real if sc > 0 else -real), (imag if ss > 0 else -imag)
+    return taken(times(re, c), times(im, s)), added(times(re, s), times(im, c))
+
+
+def forward_real(leaf, start, step, size):
+    if size == 2:
+        value = leaf(start)
+        return [(value, None), (value, None)]
+    even = forward_real(leaf, start, 2 * step, size // 2)
+    odd = forward_real(leaf, start + step, 2 * step, size // 2)
+    half, quarter = size // 2, size // 4
+    result = [None] * (half + 1)
+    for k in range(quarter + 1):
+        re, im = turned(odd[k], -2.0 * math.pi * k / size)
+        if k < quarter or quarter == 0:
+            far = (taken(even[k][0], re), times(taken(even[k][1], im), -1.0))
+            result[half - k] = far
+        result[k] = (added(even[k][0], re), added(even[k][1], im))
+    return result
+
+
+def inverse_real(spectrum, size):
+    if size == 2:
+        return [added(spectrum[0][0], spectrum[1][0])]
+    half, quarter = size // 2, size // 4
+    even, odd = [], []
+    for k in range(quarter + 1):
+        near, far = spectrum[k], spectrum[half - k]
+        if k == quarter:
+            even.append((near[0] + near[0], None))
+            odd.append((times(near[1] + near[1], -1.0), None))
+            continue
+        even.append((added(near[0], far[0]), taken(near[1], far[1])))
+        gap = (taken(near[0], far[0]), added(near[1], far[1]))
+        odd.append(turned(gap, 2.0 * math.pi * k / size))
+    firsts = inverse_real(even, half)
+    seconds = inverse_real(odd, half)
+    return [value for pair in zip(firsts, seconds) for value in pair]
+
+
+def exchange(src, dst, send, recv, place):
+    return pltpu.make_async_remote_copy(
+        src_ref=src, dst_ref=dst, send_sem=send, recv_sem=recv, device_id=place, device_id_type=MESH
+    )
+
+
+def table_product(high, low, values):
+    upper = values.astype(jnp.bfloat16)
+    lower = (values - upper.astype(jnp.float32)).astype(jnp.bfloat16)
+    wide = jnp.concatenate([upper, lower], axis=1)
+    first = jnp.dot(high, wide, preferred_element_type=jnp.float32)
+    second = jnp.dot(low, upper, preferred_element_type=jnp.float32)
+    return first[:, :LANES] + (first[:, LANES:] + second)
+
+
+def whole_kernel(
+    n, q_hbm, k_hbm, v_hbm, taps, h_hbm, skip, w_hbm, fh_hbm, fl_hbm, ih_hbm, il_hbm, out,
+    raw, h_all, fh, fl, ih, il, halo, h_send, h_recv, x_send, x_recv, y_recv, queries, direct,
+    work, spectrum, gated, weights, p_send, p_recv,
+    local_sem, w_sem, halo_s, halo_r, hs, hr, xs, xr, ys, yr, ps, pr,
+):
+    f32, bf16 = jnp.float32, jnp.bfloat16
+    y_send = h_send
+    me = lax.axis_index("ctx")
+    mine = lax.axis_index("chan")
+    other = 1 - mine
+    rows = raw.shape[1]
+    outer = 4 * n
+    half = outer // 2
+    entries = half + 1
+    group = 3 if entries % 3 == 0 else 1
+    features = out.shape[1]
+    tiles = features // TILE
+
+    def lanes_of(p):
+        return pl.ds(pl.multiple_of(p * LANES, LANES), LANES)
+
+    def weight_copy(i):
+        column = lax.rem(other + i // tiles, 2) * features + lax.rem(i, tiles) * TILE
+        slot = lax.rem(i, 2)
+        return pltpu.make_async_copy(
+            w_hbm.at[:, pl.ds(pl.multiple_of(column, TILE), TILE)], weights.at[slot], w_sem.at[slot]
+        )
+
+    sources = (h_hbm, k_hbm, v_hbm, q_hbm, fh_hbm, fl_hbm, ih_hbm, il_hbm)
+    targets = (h_all, raw.at[1], raw.at[2], raw.at[0], fh, fl, ih, il)
+    copies = [
+        pltpu.make_async_copy(src, dst, local_sem.at[i]) for i, (src, dst) in enumerate(zip(sources, targets))
+    ]
+    for copy in copies:
+        copy.start()
+    weight_copy(0).start()
+    weight_copy(1).start()
+
+    barrier = pltpu.get_barrier_semaphore()
+
+    @pl.loop(1, n)
+    def _(s):
+        pl.semaphore_signal(barrier, inc=1, device_id={"ctx": lax.rem(me + s, n)}, device_id_type=MESH)
+
+    pl.semaphore_signal(barrier, inc=1, device_id={"chan": other}, device_id_type=MESH)
+    pl.semaphore_wait(barrier, n)
+
+    after = {"ctx": lax.rem(me + 1, n)}
+    tails = [
+        exchange(src.at[pl.ds(rows - 16, 16)], halo.at[b], halo_s.at[b], halo_r.at[b], after)
+        for b, src in enumerate((q_hbm, k_hbm, v_hbm))
+    ]
+    for b in (1, 2, 0):
+        tails[b].start()
+
+    copies[0].wait()
+
+    @pl.loop(1, n)
+    def _(s):
+        p = lax.rem(me + s, n)
+        h_send[p] = h_all[:, lanes_of(p)].astype(bf16)
+        exchange(h_send.at[p], h_recv.at[me], hs.at[p], hr.at[me], {"ctx": p}).start()
+
+    h_recv[me] = h_all[:, lanes_of(me)].astype(bf16)
+
+    place = lax.broadcasted_iota(jnp.int32, (rows, LANES), 0)
+
+    def short(branch, lanes):
+        now = raw[branch, :, lanes].astype(f32)
+        before = halo[branch, :, lanes].astype(f32)
+        before = jnp.where(me > 0, before, 0.0)
+        last, former = before[15:16], before[14:15]
+        one = jnp.where(place == 0, last, pltpu.roll(now, 1, 0))
+        two = jnp.where(place == 0, former, jnp.where(place == 1, last, pltpu.roll(now, 2, 0)))
+        tap = [taps[pl.ds(3 * branch + i, 1), lanes] for i in range(3)]
+        return tap[0] * now + tap[1] * one + tap[2] * two
+
+    copies[1].wait()
+    copies[2].wait()
+    tails[1].wait_recv()
+    tails[2].wait_recv()
+
+    def mixed_of(p):
+        lanes = lanes_of(p)
+        mixed = short(1, lanes) * short(2, lanes)
+        direct[:, lanes] = skip[:, lanes] * mixed
+        return mixed.astype(bf16)
+
+    @pl.loop(1, n)
+    def _(s):
+        p = lax.rem(me + s, n)
+        x_send[p] = mixed_of(p)
+        exchange(x_send.at[p], x_recv.at[me], xs.at[p], xr.at[me], {"ctx": p}).start()
+
+    x_recv[me] = mixed_of(me)
+
+    copies[3].wait()
+    tails[0].wait_recv()
+
+    @pl.loop(0, n)
+    def _(p):
+        queries[:, lanes_of(p)] = short(0, lanes_of(p))
+
+    for copy in copies[4:]:
+        copy.wait()
+
+    def arrived(refs, p):
+        src, dst, send, recv = refs
+        return exchange(src.at[p], dst.at[p], send.at[p], recv.at[p], {"ctx": p})
+
+    def wait_all(refs):
+        @pl.loop(1, n)
+        def _(s):
+            arrived(refs, lax.rem(me + s, n)).wait_recv()
+
+    def sent_all(refs):
+        @pl.loop(1, n)
+        def _(s):
+            arrived(refs, lax.rem(me + s, n)).wait_send()
+
+    def outer_forward(received):
+        @pl.loop(0, INNER // 16)
+        def _(t):
+            for part in range(2):
+                def leaf(j):
+                    begin = pl.multiple_of((j % 2) * INNER + t * 16, 16)
+                    return received[j // 2, pl.ds(begin, 16), :].astype(f32)[part * 8 : part * 8 + 8]
+
+                begin = pl.multiple_of(t * 16 + part * 8, 8)
+                for k, (re, im) in enumerate(forward_real(leaf, 0, 1, outer)):
+                    work[k, pl.ds(begin, 8), :] = re
+                    work[k, pl.ds(INNER + begin, 8), :] = jnp.zeros((8, LANES), f32) if im is None else im
+
+    wait_all((h_send, h_recv, hs, hr))
+    outer_forward(h_recv)
+
+    @pl.loop(0, entries // group)
+    def _(g):
+        for j in range(group):
+            k = g * group + j
+            spectrum[k] = table_product(fh[k], fl[k], work[k])
+
+    wait_all((x_send, x_recv, xs, xr))
+    outer_forward(x_recv)
+
+    @pl.loop(0, entries // group)
+    def _(g):
+        for j in range(group):
+            k = g * group + j
+            x = table_product(fh[k], fl[k], work[k])
+            h = spectrum[k]
+            xre, xim, hre, him = x[:INNER], x[INNER:], h[:INNER], h[INNER:]
+            product = jnp.concatenate([xre * hre - xim * him, xre * him + xim * hre], axis=0)
+            work[k] = table_product(ih[k], il[k], product)
+
+    @pl.loop(0, INNER // 8)
+    def _(t):
+        begin = pl.multiple_of(t * 8, 8)
+        near, far = pl.ds(begin, 8), pl.ds(INNER + begin, 8)
+        bins = [(work[k, near, :], work[k, far, :] if 0 < k < half else None) for k in range(entries)]
+        for j, value in enumerate(inverse_real(bins, outer)):
+            work[j, near, :] = value
+
+    sent_all((h_send, h_recv, hs, hr))
+    scale = np.float32(1.0 / (outer * INNER))
+
+    def rows_for(ref, index, p):
+        for j in range(2):
+            ref[index, pl.ds(j * INNER, INNER), :] = (work[2 * p + j, pl.ds(0, INNER), :] * scale).astype(bf16)
+
+    @pl.loop(1, n)
+    def _(s):
+        p = lax.rem(me + s, n)
+        rows_for(y_send, p, p)
+        exchange(y_send.at[p], y_recv.at[me], ys.at[p], yr.at[me], {"ctx": p}).start()
+
+    rows_for(y_recv, me, me)
+
+    def gate(p):
+        lanes = lanes_of(p)
+        gated[:, lanes] = (queries[:, lanes] * (y_recv[p].astype(f32) + direct[:, lanes])).astype(bf16)
+
+    gate(me)
+
+    @pl.loop(1, n)
+    def _(s):
+        p = lax.rem(me - s + n, n)
+        arrived((y_send, y_recv, ys, yr), p).wait_recv()
+        gate(p)
+
+    def partial_copy(i):
+        return exchange(p_send.at[i], p_recv.at[i], ps.at[i], pr.at[i], {"chan": other})
+
+    def product_of(i):
+        weight_copy(i).wait()
+        return jnp.dot(gated[...], weights[lax.rem(i, 2)], preferred_element_type=f32)
+
+    @pl.loop(0, tiles)
+    def _(i):
+        p_send[i] = product_of(i).astype(bf16)
+        partial_copy(i).start()
+        weight_copy(i + 2).start()
+
+    @pl.loop(0, tiles)
+    def _(i):
+        own = product_of(i + tiles)
+
+        @pl.when(i + 2 < tiles)
+        def _():
+            weight_copy(i + tiles + 2).start()
+
+        partial_copy(i).wait_recv()
+        out[:, pl.ds(pl.multiple_of(i * TILE, TILE), TILE)] = (own + p_recv[i].astype(f32)).astype(bf16)
+
+    sent_all((x_send, x_recv, xs, xr))
+    sent_all((y_send, y_recv, ys, yr))
+    for tail in tails:
+        tail.wait_send()
+
+    @pl.loop(0, tiles)
+    def _(i):
+        partial_copy(i).wait_send()
+
+
+def fused_local(raw_query, raw_key, raw_value, short_filter, long_filter, skip, w_out):
+    n = lax.axis_size("ctx")
+    rows, width = raw_query.shape
+    features = w_out.shape[1] // 2
+    outer = 4 * n
+    tiles = features // TILE
+    entries = outer // 2 + 1
+    table = inner_tables(outer, INNER)
+    bf16, f32 = jnp.bfloat16, jnp.float32
+
+    def parts_of(values):
+        high = values.astype(bf16)
+        low = (values - high.astype(np.float32)).astype(bf16)
+        return jnp.asarray(high), jnp.asarray(low)
+
+    fh, fl = parts_of(table)
+    ih, il = parts_of(np.ascontiguousarray(table.transpose(0, 2, 1)))
+    anywhere = pl.BlockSpec(memory_space=pl.ANY)
+    inside = pl.BlockSpec(memory_space=pltpu.VMEM)
+    tables = pltpu.VMEM((entries, 2 * INNER, 2 * INNER), bf16)
+    blocks = pltpu.VMEM((n, rows, LANES), bf16)
+    bins = pltpu.VMEM((entries, 2 * INNER, LANES), f32)
+    dma = pltpu.SemaphoreType.DMA
+    return pl.pallas_call(
+        functools.partial(whole_kernel, n),
+        out_shape=jax.ShapeDtypeStruct((rows, features), bf16),
+        in_specs=[anywhere] * 3 + [inside, anywhere, inside] + [anywhere] * 5,
+        out_specs=inside,
+        scratch_shapes=[
+            pltpu.VMEM((3, rows, width), bf16),
+            pltpu.VMEM((rows, width), f32),
+            tables, tables, tables, tables,
+            pltpu.VMEM((3, 16, width), bf16),
+            blocks, blocks, blocks, blocks, blocks,
+            pltpu.VMEM((rows, width), f32),
+            pltpu.VMEM((rows, width), f32),
+            bins, bins,
+            pltpu.VMEM((rows, width), bf16),
+            pltpu.VMEM((2, width, TILE), bf16),
+            pltpu.VMEM((tiles, rows, TILE), bf16),
+            pltpu.VMEM((tiles, rows, TILE), bf16),
+            dma((8,)), dma((2,)), dma((3,)), dma((3,)),
+            dma((n,)), dma((n,)), dma((n,)), dma((n,)), dma((n,)), dma((n,)),
+            dma((tiles,)), dma((tiles,)),
+        ],
+        compiler_params=pltpu.CompilerParams(
+            collective_id=0, has_side_effects=True, vmem_limit_bytes=60 * 1024 * 1024
+        ),
+    )(
+        raw_query, raw_key, raw_value, short_filter.reshape(9, width), long_filter,
+        skip.reshape(1, width), w_out, fh, fl, ih, il,
+    )
+
+
+def local(*arrays):
+    rows, width = arrays[0].shape
+    n = lax.axis_size("ctx")
+    fits = lax.axis_size("chan") == 2 and rows == 2 * INNER and width == n * LANES
+    fits = fits and n & (n - 1) == 0 and n <= 16 and arrays[6].shape[1] % (4 * TILE) == 0
+    return fused_local(*arrays) if fits else plain_local(*arrays)
+
+
 def solution(mesh):
     in_specs = (
         P("ctx", "chan"),

time: 242 us -> 147 us (0.61)
  the two profiles are of different devices: /device:TPU:0 before, /device:TPU:27 now
where the time goes in v1:
time: 147 us
  Pallas kernels  142 us (97%)
  local copies, waits for them, and re-layouts  4.71 us (3%)
    pallas_call x1, Pallas kernels, fused_local(): pl.pallas_call(functools.partial(whole_kernel, n), out_shape=jax.ShapeDty...  142 us
    unnamed x1, local copies, waits for them, and re-layouts  3.13 us

profile of v1, /device:TPU:27, one launch (start us, length us, event | category | flops | bytes accessed | tf_op | source)
XLA Modules:
  0.0 147.1 jit_solution(17959084549995955459)
XLA Ops:
  0.0 1.6 %reshape.6.taps = f32[9,2048]{1,0:T(8,128)} reshape(f32[3,3,2048]{2,1,0:T(4,128)} %param.14) | data formatting | bytes 147456 | tf_op jit(solution)/shard_map/reshape | solution.py:473
  1.6 142.3 %shard_map.109 = bf16[256,4096]{1,0:T(8,128)(2,1)} custom-call(bf16[256,2048]{1,0:T(8,128)(2,1)} %q_hbm.1, bf16[256,2048]{1,0:T(8,128)(2,1)} %k_hbm.1, bf16[256,2048]{1,0:T(8,128)(2,1)} %v_hbm.1, f32[9,2048]{1,0:T(8,128)} %reshape.6.taps, f32[256,2048]{1,0:T(8,128)} %h_hbm.1, f32[1,2048]{1,0:T(1,128)} %bitcast.1, bf16[2048,8192]{1,0:T(8,128)(2,1)} %w_hbm.1, ...), custom_call_target="tpu_custom_call" | custom-call | tf_op jit(solution)/shard_map/pallas_call | solution.py:447
  143.9 3.1 %copy.13 = bf16[256,4096]{1,0:T(8,128)(2,1)} copy(bf16[256,4096]{1,0:T(8,128)(2,1)} %shard_map.109) | data formatting | bytes 4194304

commit v2 on v1

--- a/solution.py
+++ b/solution.py
@@ -110,6 +110,7 @@
 LANES = 128
 INNER = 128
 TILE = 512
+CHUNKS = 2
 
 
 def added(a, b):
@@ -211,7 +212,7 @@
     outer = 4 * n
     half = outer // 2
     entries = half + 1
-    group = 3 if entries % 3 == 0 else 1
+    group = next(size for size in (11, 3, 1) if entries % size == 0)
     features = out.shape[1]
     tiles = features // TILE
 
@@ -219,11 +220,23 @@
         return pl.ds(pl.multiple_of(p * LANES, LANES), LANES)
 
     def weight_copy(i):
-        column = lax.rem(other + i // tiles, 2) * features + lax.rem(i, tiles) * TILE
+        column = lax.rem(other + i // (CHUNKS * tiles), 2) * features + lax.rem(i, tiles) * TILE
         slot = lax.rem(i, 2)
         return pltpu.make_async_copy(
             w_hbm.at[:, pl.ds(pl.multiple_of(column, TILE), TILE)], weights.at[slot], w_sem.at[slot]
         )
+
+    side, spot, span = me // (n // 2), lax.rem(me, n // 2), n // 2
+
+    def each_peer(visit):
+        @pl.loop(0, span)
+        def _(j):
+            step = lax.rem(spot + j, span)
+            visit((1 - side) * span + step)
+
+            @pl.when(j > 0)
+            def _():
+                visit(side * span + step)
 
     sources = (h_hbm, k_hbm, v_hbm, q_hbm, fh_hbm, fl_hbm, ih_hbm, il_hbm)
     targets = (h_all, raw.at[1], raw.at[2], raw.at[0], fh, fl, ih, il)
@@ -254,9 +267,8 @@
 
     copies[0].wait()
 
-    @pl.loop(1, n)
-    def _(s):
-        p = lax.rem(me + s, n)
+    @each_peer
+    def _(p):
         h_send[p] = h_all[:, lanes_of(p)].astype(bf16)
         exchange(h_send.at[p], h_recv.at[me], hs.at[p], hr.at[me], {"ctx": p}).start()
 
@@ -271,7 +283,7 @@
         last, former = before[15:16], before[14:15]
         one = jnp.where(place == 0, last, pltpu.roll(now, 1, 0))
         two = jnp.where(place == 0, former, jnp.where(place == 1, last, pltpu.roll(now, 2, 0)))
-        tap = [taps[pl.ds(3 * branch + i, 1), lanes] for i in range(3)]
+        tap = [taps[branch, pl.ds(i, 1), lanes] for i in range(3)]
         return tap[0] * now + tap[1] * one + tap[2] * two
 
     copies[1].wait()
@@ -285,9 +297,8 @@
         direct[:, lanes] = skip[:, lanes] * mixed
         return mixed.astype(bf16)
 
-    @pl.loop(1, n)
-    def _(s):
-        p = lax.rem(me + s, n)
+    @each_peer
+    def _(p):
         x_send[p] = mixed_of(p)
         exchange(x_send.at[p], x_recv.at[me], xs.at[p], xr.at[me], {"ctx": p}).start()
 
@@ -335,88 +346,114 @@
 
     @pl.loop(0, entries // group)
     def _(g):
-        for j in range(group):
-            k = g * group + j
-            spectrum[k] = table_product(fh[k], fl[k], work[k])
+        ks = [g * group + j for j in range(group)]
+        made = [table_product(fh[k], fl[k], work[k]) for k in ks]
+        for k, value in zip(ks, made):
+            spectrum[k] = value
 
     wait_all((x_send, x_recv, xs, xr))
     outer_forward(x_recv)
 
     @pl.loop(0, entries // group)
     def _(g):
-        for j in range(group):
-            k = g * group + j
-            x = table_product(fh[k], fl[k], work[k])
+        ks = [g * group + j for j in range(group)]
+        signals = [table_product(fh[k], fl[k], work[k]) for k in ks]
+        products = []
+        for k, x in zip(ks, signals):
             h = spectrum[k]
             xre, xim, hre, him = x[:INNER], x[INNER:], h[:INNER], h[INNER:]
-            product = jnp.concatenate([xre * hre - xim * him, xre * him + xim * hre], axis=0)
-            work[k] = table_product(ih[k], il[k], product)
-
-    @pl.loop(0, INNER // 8)
-    def _(t):
-        begin = pl.multiple_of(t * 8, 8)
-        near, far = pl.ds(begin, 8), pl.ds(INNER + begin, 8)
-        bins = [(work[k, near, :], work[k, far, :] if 0 < k < half else None) for k in range(entries)]
-        for j, value in enumerate(inverse_real(bins, outer)):
-            work[j, near, :] = value
+            products.append(jnp.concatenate([xre * hre - xim * him, xre * him + xim * hre], axis=0))
+        made = [table_product(ih[k], il[k], product) for k, product in zip(ks, products)]
+        for k, value in zip(ks, made):
+            work[k] = value
 
     sent_all((h_send, h_recv, hs, hr))
     scale = np.float32(1.0 / (outer * INNER))
-
-    def rows_for(ref, index, p):
+    piece = INNER // CHUNKS
+    height = rows // CHUNKS
+
+    def rows_for(ref, index, p, q):
         for j in range(2):
-            ref[index, pl.ds(j * INNER, INNER), :] = (work[2 * p + j, pl.ds(0, INNER), :] * scale).astype(bf16)
-
-    @pl.loop(1, n)
-    def _(s):
-        p = lax.rem(me + s, n)
-        rows_for(y_send, p, p)
-        exchange(y_send.at[p], y_recv.at[me], ys.at[p], yr.at[me], {"ctx": p}).start()
-
-    rows_for(y_recv, me, me)
-
-    def gate(p):
+            value = work[2 * p + j, pl.ds(q * piece, piece), :] * scale
+            ref[index, pl.ds(q * height + j * piece, piece), :] = value.astype(bf16)
+
+    def returned(p, q, source):
+        part = pl.ds(q * height, height)
+        return exchange(
+            y_send.at[p, part], y_recv.at[source, part], ys.at[q * n + p], yr.at[q * n + source], {"ctx": p}
+        )
+
+    for q in range(CHUNKS):
+        @pl.loop(q * (piece // 8), (q + 1) * (piece // 8))
+        def _(t):
+            begin = pl.multiple_of(t * 8, 8)
+            near, far = pl.ds(begin, 8), pl.ds(INNER + begin, 8)
+            bins = [(work[k, near, :], work[k, far, :] if 0 < k < half else None) for k in range(entries)]
+            for j, value in enumerate(inverse_real(bins, outer)):
+                work[j, near, :] = value
+
+        @each_peer
+        def _(p):
+            rows_for(y_send, p, p, q)
+            returned(p, q, me).start()
+
+        rows_for(y_recv, me, me, q)
+
+    def gate(p, q):
         lanes = lanes_of(p)
-        gated[:, lanes] = (queries[:, lanes] * (y_recv[p].astype(f32) + direct[:, lanes])).astype(bf16)
-
-    gate(me)
-
-    @pl.loop(1, n)
-    def _(s):
-        p = lax.rem(me - s + n, n)
-        arrived((y_send, y_recv, ys, yr), p).wait_recv()
-        gate(p)
+        for j in range(2):
+            there, here = pl.ds(j * INNER + q * piece, piece), pl.ds(q * height + j * piece, piece)
+            sum_of = y_recv[p, here, :].astype(f32) + direct[there, lanes]
+            gated[here, lanes] = (queries[there, lanes] * sum_of).astype(bf16)
 
     def partial_copy(i):
         return exchange(p_send.at[i], p_recv.at[i], ps.at[i], pr.at[i], {"chan": other})
 
-    def product_of(i):
-        weight_copy(i).wait()
-        return jnp.dot(gated[...], weights[lax.rem(i, 2)], preferred_element_type=f32)
+    for q in range(CHUNKS):
+        gate(me, q)
+
+        @each_peer
+        def _(p):
+            returned(p, q, p).wait_recv()
+            gate(p, q)
+
+        @pl.loop(q * tiles, (q + 1) * tiles)
+        def _(i):
+            weight_copy(i).wait()
+            left = gated[pl.ds(q * height, height), :]
+            part = jnp.dot(left, weights[lax.rem(i, 2)], preferred_element_type=f32)
+            p_send[i] = part.astype(bf16)
+            partial_copy(i).start()
+            weight_copy(i + 2).start()
 
     @pl.loop(0, tiles)
     def _(i):
-        p_send[i] = product_of(i).astype(bf16)
-        partial_copy(i).start()
-        weight_copy(i + 2).start()
-
-    @pl.loop(0, tiles)
-    def _(i):
-        own = product_of(i + tiles)
+        number = i + CHUNKS * tiles
+        weight_copy(number).wait()
+        own = jnp.dot(gated[...], weights[lax.rem(number, 2)], preferred_element_type=f32)
 
         @pl.when(i + 2 < tiles)
         def _():
-            weight_copy(i + tiles + 2).start()
-
-        partial_copy(i).wait_recv()
-        out[:, pl.ds(pl.multiple_of(i * TILE, TILE), TILE)] = (own + p_recv[i].astype(f32)).astype(bf16)
+            weight_copy(number + 2).start()
+
+        columns = pl.ds(pl.multiple_of(i * TILE, TILE), TILE)
+        for q in range(CHUNKS):
+            partial_copy(q * tiles + i).wait_recv()
+            for j in range(2):
+                begin = q * height + j * piece
+                came = p_recv[q * tiles + i, pl.ds(j * piece, piece), :].astype(f32)
+                out[pl.ds(j * INNER + q * piece, piece), columns] = (own[begin : begin + piece] + came).astype(bf16)
 
     sent_all((x_send, x_recv, xs, xr))
-    sent_all((y_send, y_recv, ys, yr))
+    for q in range(CHUNKS):
+        @each_peer
+        def _(p):
+            returned(p, q, me).wait_send()
+
     for tail in tails:
         tail.wait_send()
 
-    @pl.loop(0, tiles)
+    @pl.loop(0, CHUNKS * tiles)
     def _(i):
         partial_copy(i).wait_send()
 
@@ -460,17 +497,17 @@
             bins, bins,
             pltpu.VMEM((rows, width), bf16),
             pltpu.VMEM((2, width, TILE), bf16),
-            pltpu.VMEM((tiles, rows, TILE), bf16),
-            pltpu.VMEM((tiles, rows, TILE), bf16),
+            pltpu.VMEM((CHUNKS * tiles, rows // CHUNKS, TILE), bf16),
+            pltpu.VMEM((CHUNKS * tiles, rows // CHUNKS, TILE), bf16),
             dma((8,)), dma((2,)), dma((3,)), dma((3,)),
-            dma((n,)), dma((n,)), dma((n,)), dma((n,)), dma((n,)), dma((n,)),
-            dma((tiles,)), dma((tiles,)),
+            dma((n,)), dma((n,)), dma((n,)), dma((n,)), dma((CHUNKS * n,)), dma((CHUNKS * n,)),
+            dma((CHUNKS * tiles,)), dma((CHUNKS * tiles,)),
         ],
         compiler_params=pltpu.CompilerParams(
             collective_id=0, has_side_effects=True, vmem_limit_bytes=60 * 1024 * 1024
         ),
     )(
-        raw_query, raw_key, raw_value, short_filter.reshape(9, width), long_filter,
+        raw_query, raw_key, raw_value, short_filter, long_filter,
         skip.reshape(1, width), w_out, fh, fl, ih, il,
     )
 

time: 147 us -> 133 us (0.905)
  the two profiles are of different devices: /device:TPU:27 before, /device:TPU:0 now
where the time goes in v2:
time: 133 us
  Pallas kernels  130 us (98%)
  local copies, waits for them, and re-layouts  3.13 us (2%)
    pallas_call x1, Pallas kernels, fused_local(): pl.pallas_call(functools.partial(whole_kernel, n), out_shape=jax.ShapeDty...  130 us
    unnamed x1, local copies, waits for them, and re-layouts  3.13 us

profile of v2, /device:TPU:0, one launch (start us, length us, event | category | flops | bytes accessed | tf_op | source)
XLA Modules:
  0.0 132.9 jit_solution(9784004943983081929)
XLA Ops:
  0.0 129.8 %shard_map.109 = bf16[256,4096]{1,0:T(8,128)(2,1)} custom-call(bf16[256,2048]{1,0:T(8,128)(2,1)} %q_hbm.1, bf16[256,2048]{1,0:T(8,128)(2,1)} %k_hbm.1, bf16[256,2048]{1,0:T(8,128)(2,1)} %v_hbm.1, f32[3,3,2048]{2,1,0:T(4,128)} %taps.1, f32[256,2048]{1,0:T(8,128)} %h_hbm.1, f32[1,2048]{1,0:T(1,128)} %bitcast.1, bf16[2048,8192]{1,0:T(8,128)(2,1)} %w_hbm.1, ...), custom_call_target="tpu_custom_call" | custom-call | tf_op jit(solution)/shard_map/pallas_call | solution.py:484
  129.8 3.1 %copy.13 = bf16[256,4096]{1,0:T(8,128)(2,1)} copy(bf16[256,4096]{1,0:T(8,128)(2,1)} %shard_map.109) | data formatting | bytes 4194304

commit v3 on v2

--- a/solution.py
+++ b/solution.py
@@ -110,7 +110,7 @@
 LANES = 128
 INNER = 128
 TILE = 512
-CHUNKS = 2
+CHUNKS = 4
 
 
 def added(a, b):

time: 133 us -> 128 us (0.962)
  Pallas kernels: 130 us -> 124 us
    pallas_call x1, Pallas kernels: 130 us -> 124 us  [fused_local(): pl.pallas_call(functools.partial(whole_kernel, n), out_shape=jax.ShapeDty...]
where the time goes in v3:
time: 128 us; the launch traced here: 127 us
  Pallas kernels  124 us (97%)
  local copies, waits for them, and re-layouts  3.13 us (2%)
    pallas_call x1, Pallas kernels, fused_local(): pl.pallas_call(functools.partial(whole_kernel, n), out_shape=jax.ShapeDty...  124 us
    unnamed x1, local copies, waits for them, and re-layouts  3.13 us

profile of v3, /device:TPU:0, one launch (start us, length us, event | category | flops | bytes accessed | tf_op | source)
XLA Modules:
  0.0 127.0 jit_solution(13827351918162235524)
XLA Ops:
  0.0 123.9 %shard_map.109 = bf16[256,4096]{1,0:T(8,128)(2,1)} custom-call(bf16[256,2048]{1,0:T(8,128)(2,1)} %q_hbm.1, bf16[256,2048]{1,0:T(8,128)(2,1)} %k_hbm.1, bf16[256,2048]{1,0:T(8,128)(2,1)} %v_hbm.1, f32[3,3,2048]{2,1,0:T(4,128)} %taps.1, f32[256,2048]{1,0:T(8,128)} %h_hbm.1, f32[1,2048]{1,0:T(1,128)} %bitcast.1, bf16[2048,8192]{1,0:T(8,128)(2,1)} %w_hbm.1, ...), custom_call_target="tpu_custom_call" | custom-call | tf_op jit(solution)/shard_map/pallas_call | solution.py:484
  123.9 3.1 %copy.13 = bf16[256,4096]{1,0:T(8,128)(2,1)} copy(bf16[256,4096]{1,0:T(8,128)(2,1)} %shard_map.109) | data formatting | bytes 4194304
